TPU v7x, 32 devices: a whole 2x2x4 slice. The times are simulated.
32 devices in a mesh: slab: 8 (over y, x, core), tomo: 4 (over z).
Axes of the slice: x: 2, y: 2, z: 4, core: 2. Of those that a mesh axis runs over, the one named last changes fastest.
Arguments:
- tomogram: bfloat16 [4, 128, 256, 256], P('tomo', 'slab'), may hold values from -6 to 6
- centers: int32 [4, 3, 256], P('tomo', None, 'slab'), may hold values from 0 to 240, as said below
- owner: int32 [4, 256], P('tomo', 'slab'), may hold values from -1 to 7, as said below
- rotation: int32 [4, 256], P('tomo', 'slab'), may hold values from 0 to 31
- ctf: float32 [4, 32, 1024], P('tomo'), may hold values from -1 to 1
- ref_spectra: float32 [32, 2, 32, 1024], replicated, may hold values from -6 to 6
Outputs:
- score: float32 [4, 128], P('tomo', 'slab')
- new_reference: float32 [32, 2, 32, 1024], replicated
Inputs may be any that keep to these rules, and one draw needn't show every extreme that they name: The z center of a slot held by slab index s lies in [s * 16, (s + 1) * 16); x centers lie in [16, 240] and y centers in [16, 240]. Among the slots held by one slab index, each owner is named by 0 or exactly 4 slots; each owner is named by exactly 16 slots of its tomogram.
All inputs are finite; a program needn't handle non-finite values.
Results may differ from a plain program's by a relative error of at most 0.0003.
Values may be sent and summed in bfloat16 or wider, within the bound.
A program may use at most 320 MiB of HBM per device.

v0:
```python
import math

import jax
import jax.numpy as jnp
from jax import lax
from jax.sharding import PartitionSpec as P

P_DEV = 16


pass_forms = ("pqkn,sqnab->spkab", "pqkn,sqanb->spakb", "pqkn,sqabn->spabk")


def with_halo(cells, sides, width):
    for axis, dim in sides:
        count = lax.axis_size(axis)
        ends = count - 1
        head = lax.slice_in_dim(cells, 0, width, axis=dim)
        tail = lax.slice_in_dim(cells, cells.shape[dim] - width, cells.shape[dim], axis=dim)
        cells = jnp.concatenate(
            [
                lax.ppermute(tail, axis, [(i, (i + 1) % count) for i in range(ends)]),
                cells,
                lax.ppermute(head, axis, [((i + 1) % count, i) for i in range(ends)]),
            ],
            axis=dim,
        )
    return cells


def dft_tables(length, direction):
    positions = jnp.arange(length, dtype=jnp.int32)
    angles = (
        2.0
        * math.pi
        / length
        * (positions[:, None] * positions[None, :] % length).astype(jnp.float32)
    )
    norm_scale = 1.0 / math.sqrt(length)
    cosine = jnp.cos(angles) * norm_scale
    sine_table = jnp.sin(angles) * norm_scale
    first_row = jnp.stack((cosine, direction * sine_table), axis=0)
    second_row = jnp.stack((-direction * sine_table, cosine), axis=0)
    return jnp.stack((first_row, second_row), axis=0)


def transform_real(real_part, table):
    slots, box_len = (real_part.shape[0], real_part.shape[1])
    flat = real_part.reshape(slots, 1, box_len, box_len * box_len)
    state = jnp.einsum("pqkn,sqnm->spkm", table[:, :1], flat, precision=lax.Precision.HIGH)
    state = state.reshape(slots, 2, box_len, box_len, box_len)
    for einsum_form in pass_forms[1:]:
        state = jnp.einsum(einsum_form, table, state, precision=lax.Precision.HIGH)
    return state


def transform_complex(state, table):
    slots, box_len = (state.shape[0], state.shape[2])
    flat = state.reshape(slots, 2, box_len, box_len * box_len)
    state = jnp.einsum("pqkn,sqnm->spkm", table, flat, precision=lax.Precision.HIGH)
    state = state.reshape(slots, 2, box_len, box_len, box_len)
    for einsum_form in pass_forms[1:]:
        state = jnp.einsum(einsum_form, table, state, precision=lax.Precision.HIGH)
    return state


def local(tomogram, centers, owner, rotation, ctf, ref_spectra):
    slab_count = lax.axis_size("slab")
    box_len = ref_spectra.shape[2]
    half_box = box_len // 2
    cell_count = box_len**3
    ref_count = ref_spectra.shape[0]
    slab_depth = tomogram.shape[1]
    capacity = 2 * P_DEV // slab_count
    slot_count = owner.shape[1]
    buffer_len = slab_count * capacity
    padded = with_halo(tomogram, (("slab", 1),), half_box)
    volume = padded[0]
    depth_local = centers[0, 0] - lax.axis_index("slab") * slab_depth

    def cut_box(depth_at, row_at, col_at):
        return lax.dynamic_slice(
            volume, (depth_at, row_at - half_box, col_at - half_box), (box_len, box_len, box_len)
        )

    boxes = jax.vmap(cut_box)(depth_local, centers[0, 1], centers[0, 2])
    owners = owner[0]
    owner_hits = (owners[:, None] == jnp.arange(slab_count, dtype=jnp.int32)[None, :]).astype(
        jnp.int32
    )
    earlier = jnp.cumsum(owner_hits, axis=0) - owner_hits
    slot_rank = jnp.sum(earlier * owner_hits, axis=1)
    target = jnp.where(owners >= 0, owners * capacity + slot_rank, buffer_len)
    slot_table = (
        jnp.zeros((buffer_len + 1,), jnp.int32)
        .at[target]
        .set(jnp.arange(slot_count, dtype=jnp.int32))[:buffer_len]
    )
    filled = jnp.zeros((buffer_len + 1,), jnp.int32).at[target].set(1)[:buffer_len]
    outgoing = boxes[slot_table].reshape(slab_count, capacity, box_len, box_len * box_len)
    slot_labels = (
        jnp.where(filled > 0, rotation[0][slot_table] + 1, 0)
        .astype(jnp.bfloat16)
        .reshape(slab_count, capacity)
    )
    arrived, arrived_tags = (
        lax.all_to_all(outgoing, "slab", split_axis=0, concat_axis=0, tiled=True),
        lax.all_to_all(slot_labels, "slab", split_axis=0, concat_axis=0, tiled=True),
    )
    arrived = arrived.reshape(buffer_len, box_len, box_len, box_len)
    arrived_tags = arrived_tags.reshape(buffer_len).astype(jnp.float32)
    is_live = arrived_tags > 0.5
    rotations = jnp.maximum(arrived_tags - 1.0, 0.0).astype(jnp.int32)
    live_order = jnp.argsort(jnp.where(is_live, 0, 1).astype(jnp.int32), stable=True)[:P_DEV]
    forward_table = dft_tables(box_len, 1.0)
    inverse_table = dft_tables(box_len, -1.0)
    ref_real = ref_spectra[:, 0].reshape(ref_count, box_len, box_len, box_len)
    ref_imag = ref_spectra[:, 1].reshape(ref_count, box_len, box_len, box_len)
    ref_power = jnp.sum(ref_real * ref_real + ref_imag * ref_imag, axis=(1, 2, 3))
    weights_grid = ctf[0].reshape(box_len, box_len, box_len)
    block_size = 16
    work_boxes = arrived[live_order]
    block_total = work_boxes.shape[0] // block_size

    def block_step(carry_in, block_inputs):
        sum_real, sum_imag, counts = carry_in
        block_boxes, block_rot, block_live = block_inputs
        spec_state = (
            transform_real(block_boxes.astype(jnp.float32), forward_table)
            * weights_grid[None, None]
        )
        spec_real = spec_state[:, 0]
        spec_imag = spec_state[:, 1]
        sel_real = ref_real[block_rot]
        sel_imag = ref_imag[block_rot]
        prod_real = spec_real * sel_real + spec_imag * sel_imag
        prod_imag = spec_imag * sel_real - spec_real * sel_imag
        cross_state = transform_complex(jnp.stack((prod_real, prod_imag), axis=1), inverse_table)
        peak_value = jnp.max(cross_state[:, 0], axis=(1, 2, 3))
        own_power = jnp.sum(spec_real * spec_real + spec_imag * spec_imag, axis=(1, 2, 3))
        scores_block = cell_count * peak_value / jnp.sqrt(own_power * ref_power[block_rot] + 1e-06)
        members = (block_rot[:, None] == jnp.arange(ref_count, dtype=jnp.int32)[None, :]).astype(
            jnp.float32
        ) * block_live[:, None]
        sum_real = sum_real + jnp.einsum(
            "sr,sabc->rabc", members, spec_real, precision=lax.Precision.HIGH
        )
        sum_imag = sum_imag + jnp.einsum(
            "sr,sabc->rabc", members, spec_imag, precision=lax.Precision.HIGH
        )
        counts = counts + jnp.sum(members, axis=0)
        return ((sum_real, sum_imag, counts), scores_block)

    start = (
        jnp.zeros((ref_count, box_len, box_len, box_len), jnp.float32),
        jnp.zeros((ref_count, box_len, box_len, box_len), jnp.float32),
        jnp.zeros((ref_count,), jnp.float32),
    )
    block_inputs = (
        work_boxes.reshape(block_total, block_size, box_len, box_len, box_len),
        rotations[live_order].reshape(block_total, block_size),
        jnp.ones((P_DEV,), jnp.float32).reshape(block_total, block_size),
    )
    sums_out, scores = lax.scan(block_step, start, block_inputs)
    (num_real, num_imag, counts), aligned = (sums_out, scores.reshape(-1))
    local_weight = counts[:, None] * (ctf[0] * ctf[0]).reshape(1, cell_count)
    num_real, num_imag, denominator = lax.psum((num_real, num_imag, local_weight), ("slab", "tomo"))
    stacked = jnp.stack((num_real, num_imag), axis=1).reshape(
        ref_count, 2, box_len, box_len * box_len
    )
    new_reference = stacked / (denominator.reshape(ref_count, 1, box_len, box_len * box_len) + 1.0)
    return (aligned.reshape(1, P_DEV), new_reference)


def solution(mesh):
    return jax.shard_map(
        local,
        mesh=mesh,
        in_specs=(
            P("tomo", "slab", None, None),
            P("tomo", None, "slab"),
            P("tomo", "slab"),
            P("tomo", "slab"),
            P("tomo", None, None),
            P(),
        ),
        out_specs=(P("tomo", "slab"), P()),
        check_vma=False,
    )
```

profile of v0, /device:TPU:15, one launch (start us, length us, event | category | flops | bytes accessed | tf_op | source)
XLA Modules:
  0.0 685.5 jit_solution(11872917363848199433)
XLA Ops:
  16.3 5.7 all-to-all-start.1
  25.6 32.0 %all-to-all-done.1 = bf16[8,1,4]{2,1,0:T(2,128)(2,1)S(1)} async-done(((bf16[8,1,4]{2,1,0:T(2,128)(2,1)}), bf16[8,1,4]{2,1,0:T(2,128)(2,1)S(1)}, u32[]{:S(2)}, u32[]{:S(2)}) %all-to-all-start.1) | async-done | bytes 96 | tf_op jit(solution)/shard_map/all_to_all | solution.py:108
  65.8 144.0 %while.1 = (s32[]{:T(128)}, bf16[48,256,256]{2,1,0:T(8,128)(2,1)}, s32[32,3]{0,1:T(4,128)S(1)}, bf16[32,32,32,32]{3,2,1,0:T(8,128)(2,1)}, s32[]{:T(128)}) while((s32[]{:T(128)}, bf16[48,256,256]{2,1,0:T(8,128)(2,1)}, s32[32,3]{0,1:T(4,128)S(1)}, bf16[32,32,32,32]{3,2,1,0:T(8,128)(2,1)}, s32[]{:T(128)}) %tuple.40), condition=%wide.while_cond, body=%wide.while_body.sunk | while | flops 2 | bytes 525949 | solution.py:82
  209.8 8.3 %gather_fusion = bf16[32,32,32,32]{3,2,1,0:T(8,128)(2,1)} fusion(bf16[32,32,32,32]{3,2,1,0:T(8,128)(2,1)} %get-tuple-element.37, s32[1024]{0:T(1024)S(1)} %pad_clamp_fusion.2), kind=kCustom, calls=%fused_computation | custom fusion | bytes 4194432 | tf_op jit(solution)/shard_map/gather | solution.py:100
  218.1 12.4 %reshape.371 = bf16[8,4,32,1024]{3,2,1,0:T(8,128)(2,1)} reshape(bf16[32,32,32,32]{3,2,1,0:T(8,128)(2,1)} %gather_fusion) | data formatting | bytes 4194304 | tf_op jit(solution)/shard_map/reshape | solution.py:100
  238.0 21.3 %all-to-all-done = bf16[8,4,32,1024]{3,2,1,0:T(8,128)(2,1)S(1)} async-done(((bf16[8,4,32,1024]{3,2,1,0:T(8,128)(2,1)}), bf16[8,4,32,1024]{3,2,1,0:T(8,128)(2,1)S(1)}, u32[]{:S(2)}, u32[]{:S(2)}) %all-to-all-start) | async-done | bytes 2097184 | tf_op jit(solution)/shard_map/all_to_all | solution.py:107
  259.3 7.8 %reshape.372 = bf16[32,32,32,32]{3,2,1,0:T(8,128)(2,1)} reshape(bf16[8,4,32,1024]{3,2,1,0:T(8,128)(2,1)S(1)} %all-to-all-done) | data formatting | bytes 4194304 | tf_op jit(solution)/shard_map/reshape | solution.py:110
  267.1 6.4 gather_fusion.2
  273.4 6.2 reshape.476
  283.4 11.7 %reshape.375 = f32[16,2,32,32,32]{4,3,2,1,0:T(8,128)} reshape(f32[16,2,32,1024]{3,2,1,0:T(8,128)} %convolution_bitcast_fusion) | data formatting | bytes 8388608 | tf_op jit(solution)/shard_map/while/body/eval_jaxpr/reshape | solution.py:51
  295.1 18.2 %fusion.7 = f32[16,32,32,2,32,1]{4,2,5,3,1,0:T(8,128)} fusion(f32[16,2,32,32,32]{4,3,2,1,0:T(8,128)} %reshape.375, f32[1,2,32,32]{3,2,0,1:T(8,128)S(1)} %get-tuple-element.79, f32[1,2,32,32]{3,2,0,1:T(8,128)S(1)} %get-tuple-element.82), kind=kOutput, calls=%fused_computation.19 | convolution fusion | flops 402657280 | bytes 8404992 | tf_op jit(solution)/shard_map/while/body/eval_jaxpr/pqkn,sqanb->spakb/dot_general | solution.py:53
  313.3 16.4 %fusion = f32[16,2,32,32,32]{4,3,1,2,0:T(8,128)S(1)} fusion(f32[16,32,32,2,32,1]{4,2,5,3,1,0:T(8,128)} %fusion.7, f32[32,32,32]{2,1,0:T(8,128)S(1)} %mul.302, f32[1,2,32,32]{3,2,0,1:T(8,128)S(1)} %get-tuple-element.79, f32[1,2,32,32]{3,2,0,1:T(8,128)S(1)} %get-tuple-element.82), kind=kOutput, calls=%fused_computation.12 | convolution fusion | flops 403705856 | bytes 8536064 | tf_op jit(solution)/shard_map/while/body/eval_jaxpr/pqkn,sqabn->spabk/dot_general | solution.py:53
  329.7 7.3 %slice_bitcast_fusion.1 = (f32[16,32,32,32]{3,2,1,0:T(8,128)}, f32[16,32,32,32]{3,2,1,0:T(8,128)}) fusion(f32[16,2,32,32,32]{4,3,1,2,0:T(8,128)S(1)} %fusion), kind=kLoop, calls=%fused_computation.36 | loop fusion | bytes 8388608 | tf_op jit(solution)/shard_map/while/body/eval_jaxpr/squeeze | solution.py:132
  340.4 13.8 %fusion.16 = f32[32,32,32,32]{3,0,2,1:T(8,128)S(1)} fusion(f32[16,32,32,32]{3,2,1,0:T(8,128)} %get-tuple-element.74, s32[16]{0:T(128)S(1)} %gather_fusion.3), kind=kOutput, calls=%fused_computation.30 | convolution fusion | flops 100664320 | bytes 6291520 | tf_op jit(solution)/shard_map/while/body/eval_jaxpr/sr,sabc->rabc/dot_general | solution.py:148
  354.2 19.9 %copy.45 = f32[32,32,32,32]{3,2,1,0:T(8,128)} copy(f32[32,32,32,32]{3,0,2,1:T(8,128)S(1)} %fusion.16) | data formatting | bytes 8388608 | tf_op jit(solution)/shard_map/while/body/eval_jaxpr/sr,sabc->rabc/dot_general | solution.py:148
  374.1 13.7 %stack.73 = f32[32,1,32,1024]{3,2,0,1:T(8,128)} reshape(f32[32,32,32,32]{3,2,1,0:T(8,128)} %copy.45) | data formatting | bytes 8388608 | tf_op jit(solution)/shard_map/stack | solution.py:168
  387.7 13.9 %fusion.18 = f32[32,32,32,32]{3,0,2,1:T(8,128)S(1)} fusion(f32[16,32,32,32]{3,2,1,0:T(8,128)} %get-tuple-element.73, s32[16]{0:T(128)S(1)} %gather_fusion.3), kind=kOutput, calls=%fused_computation.32 | convolution fusion | flops 100664320 | bytes 6291520 | tf_op jit(solution)/shard_map/while/body/eval_jaxpr/sr,sabc->rabc/dot_general | solution.py:145
  401.7 19.3 %copy.43 = f32[32,32,32,32]{3,2,1,0:T(8,128)} copy(f32[32,32,32,32]{3,0,2,1:T(8,128)S(1)} %fusion.18) | data formatting | bytes 8388608 | tf_op jit(solution)/shard_map/while/body/eval_jaxpr/sr,sabc->rabc/dot_general | solution.py:145
  421.0 13.8 %stack.72 = f32[32,1,32,1024]{3,2,0,1:T(8,128)} reshape(f32[32,32,32,32]{3,2,1,0:T(8,128)} %copy.43) | data formatting | bytes 8388608 | tf_op jit(solution)/shard_map/stack | solution.py:168
  434.8 7.7 %fusion.69 = (f32[32,1,32,1024]{3,2,1,0:T(8,128)}, f32[32]{0:T(128)S(1)}, f32[32,1,32,1024]{3,2,1,0:T(8,128)}) fusion(f32[32,2,32,1024]{3,2,1,0:T(8,128)} %param.11), kind=kLoop, calls=%fused_computation.127 | loop fusion | flops 4194272 | bytes 16777344 | tf_op jit(solution)/shard_map/slice | solution.py:117
  442.5 11.8 %reshape_squeeze.7 = f32[32,32,32,32]{3,2,1,0:T(8,128)} reshape(f32[32,1,32,1024]{3,2,1,0:T(8,128)} %get-tuple-element.77) | data formatting | bytes 8388608 | tf_op jit(solution)/shard_map/reshape;squeeze | solution.py:118
  454.3 11.7 %reshape_squeeze.6 = f32[32,32,32,32]{3,2,1,0:T(8,128)} reshape(f32[32,1,32,1024]{3,2,1,0:T(8,128)} %get-tuple-element.75) | data formatting | bytes 8388608 | tf_op jit(solution)/shard_map/reshape;squeeze | solution.py:117
  466.7 11.0 %gather_fusion.5 = f32[16,32,32,32]{3,2,1,0:T(8,128)} fusion(f32[32,32,32,32]{3,2,1,0:T(8,128)} %reshape_squeeze.7, s32[1024]{0:T(1024)S(1)} %pad_clamp_fusion), kind=kCustom, calls=%fused_computation.5 | custom fusion | bytes 4194368 | tf_op jit(solution)/shard_map/while/body/eval_jaxpr/gather | solution.py:135
  477.7 10.4 %gather_fusion.4 = f32[16,32,32,32]{3,2,1,0:T(8,128)} fusion(f32[32,32,32,32]{3,2,1,0:T(8,128)} %reshape_squeeze.6, s32[1024]{0:T(1024)S(1)} %pad_clamp_fusion), kind=kCustom, calls=%fused_computation.4 | custom fusion | bytes 4194368 | tf_op jit(solution)/shard_map/while/body/eval_jaxpr/gather | solution.py:134
  488.1 19.8 %fusion.14 = (f32[16,1,32,32,32]{4,3,2,0,1:T(8,128)}, f32[16,1,32,32,32]{4,3,2,0,1:T(8,128)}) fusion(f32[16,32,32,32]{3,2,1,0:T(8,128)} %gather_fusion.5, f32[16,32,32,32]{3,2,1,0:T(8,128)} %gather_fusion.4, f32[16,2,32,32,32]{4,3,1,2,0:T(8,128)} %copy-done.2), kind=kLoop, calls=%fused_computation.26 | loop fusion | flops 3145728 | bytes 12582912 | tf_op jit(solution)/shard_map/while/body/eval_jaxpr/add | solution.py:136
  507.9 6.8 stack.65
  514.7 7.7 %stack.64 = f32[16,1,32,1024]{3,2,0,1:T(8,128)} reshape(f32[16,1,32,32,32]{4,3,2,0,1:T(8,128)} %get-tuple-element.71) | data formatting | bytes 4194304 | tf_op jit(solution)/shard_map/while/body/eval_jaxpr/stack | solution.py:138
  522.5 6.6 fusion.23
  529.1 11.6 %reshape.376 = f32[16,2,32,32,32]{4,3,2,1,0:T(8,128)} reshape(f32[16,2,32,1024]{3,2,1,0:T(8,128)} %fusion.23) | data formatting | bytes 8388608 | tf_op jit(solution)/shard_map/while/body/eval_jaxpr/reshape | solution.py:61
  540.7 18.4 %fusion.5 = f32[16,32,32,2,32,1]{4,2,5,3,1,0:T(8,128)} fusion(f32[1,2,32,32]{3,2,1,0:T(8,128)S(1)} %copy-done.6, f32[1,2,32,32]{3,2,1,0:T(8,128)S(1)} %copy-done.5, f32[16,2,32,32,32]{4,3,2,1,0:T(8,128)} %reshape.376), kind=kOutput, calls=%fused_computation.17 | convolution fusion | flops 402657280 | bytes 8404992 | tf_op jit(solution)/shard_map/while/body/eval_jaxpr/pqkn,sqanb->spakb/dot_general | solution.py:63
  559.1 18.4 %fusion.11 = f32[16,2,32,32,32]{4,3,1,2,0:T(8,128)} fusion(f32[16,32,32,2,32,1]{4,2,5,3,1,0:T(8,128)} %fusion.5, f32[1,2,32,32]{3,2,1,0:T(8,128)S(1)} %copy-done.6, f32[1,2,32,32]{3,2,1,0:T(8,128)S(1)} %copy-done.5), kind=kOutput, calls=%fused_computation.21 | convolution fusion | flops 402657280 | bytes 8404992 | tf_op jit(solution)/shard_map/while/body/eval_jaxpr/pqkn,sqabn->spabk/dot_general | solution.py:63
  584.6 82.8 %all-reduce.3.cloned.1.call-done = (f32[32,1,32,1024]{3,2,0,1:T(8,128)}, f32[32,1,32,1024]{3,2,0,1:T(8,128)}, f32[32,32768]{1,0:T(8,128)}) async-done(((f32[32,1,32,1024]{3,2,0,1:T(8,128)}, f32[32,1,32,1024]{3,2,0,1:T(8,128)}, f32[32,32768]{1,0:T(8,128)}), (f32[32,1,32,1024]{3,2,0,1:T(8,128)}, f32[32,1,32,1024]{3,2,0,1:T(8,128)}, f32[32,32768]{1,0:T(8,128)})) %all-reduce.3.cloned.1.call-update) | async-done | bytes 12582928 | tf_op jit(solution)/shard_map/psum | solution.py:167
  (170 shorter events, 198.2 us)
Async XLA Ops:
  7.2 7.7 %copy-start = (s32[1,32]{1,0:T(1,128)S(1)}, s32[1,32]{1,0:T(1,128)}, u32[]{:S(2)}) copy-start(s32[1,32]{1,0:T(1,128)} %param.9) | copy-start | bytes 388
  7.2 53.0 %collective-permute-start.1 = (bf16[1,16,256,256]{3,2,1,0:T(8,128)(2,1)}, bf16[1,16,256,256]{3,2,1,0:T(8,128)(2,1)S(1)}, u32[]{:S(2)}, u32[]{:S(2)}) collective-permute-start(bf16[1,16,256,256]{3,2,1,0:T(8,128)(2,1)} %param.6), channel_id=1, source_target_pairs={{4,0},{8,4},{12,8},{16,12},{20,16},{24,20},{28,24},{5,1},{9,5},{13... | collective-permute-start | bytes 6291464 | tf_op jit(solution)/shard_map/ppermute | solution.py:24
  9.9 50.3 %collective-permute-start = (bf16[1,16,256,256]{3,2,1,0:T(8,128)(2,1)}, bf16[1,16,256,256]{3,2,1,0:T(8,128)(2,1)}, u32[]{:S(2)}, u32[]{:S(2)}) collective-permute-start(bf16[1,16,256,256]{3,2,1,0:T(8,128)(2,1)} %param.6), channel_id=1, source_target_pairs={{0,4},{4,8},{8,12},{12,16},{16,20},{20,24},{24,28},{1,5},{5,9},{9,... | collective-permute-start | bytes 6291464 | tf_op jit(solution)/shard_map/ppermute | solution.py:22
  16.3 41.3 %all-to-all-start.1 = ((bf16[8,1,4]{2,1,0:T(2,128)(2,1)}), bf16[8,1,4]{2,1,0:T(2,128)(2,1)S(1)}, u32[]{:S(2)}, u32[]{:S(2)}) async-start(bf16[8,1,4]{2,1,0:T(2,128)(2,1)} %convert_element_type.71), calls=%async_computation.1 | async-start | bytes 8192 | tf_op jit(solution)/shard_map/all_to_all | solution.py:108
  230.5 28.8 %all-to-all-start = ((bf16[8,4,32,1024]{3,2,1,0:T(8,128)(2,1)}), bf16[8,4,32,1024]{3,2,1,0:T(8,128)(2,1)S(1)}, u32[]{:S(2)}, u32[]{:S(2)}) async-start(bf16[8,4,32,1024]{3,2,1,0:T(8,128)(2,1)} %reshape.371), calls=%async_computation | async-start | bytes 4194304 | tf_op jit(solution)/shard_map/all_to_all | solution.py:107
  235.3 432.1 %all-reduce.3.cloned.1.call-start = ((), (), s32[]{:S(2)}) async-start(), calls=%async_computation.2 | async-start | bytes 25165824 | tf_op jit(solution)/shard_map/psum | solution.py:167
  329.7 10.7 %copy-start.2 = (f32[16,2,32,32,32]{4,3,1,2,0:T(8,128)}, f32[16,2,32,32,32]{4,3,1,2,0:T(8,128)S(1)}, u32[]{:S(2)}) copy-start(f32[16,2,32,32,32]{4,3,1,2,0:T(8,128)S(1)} %fusion) | copy-start | bytes 12582916
  507.9 14.6 %copy-start.5 = (f32[1,2,32,32]{3,2,1,0:T(8,128)S(1)}, f32[1,2,32,32]{3,2,1,0:T(8,128)}, u32[]{:S(2)}) copy-start(f32[1,2,32,32]{3,2,1,0:T(8,128)} %get-tuple-element.78) | copy-start | bytes 24580
  507.9 14.6 %copy-start.6 = (f32[1,2,32,32]{3,2,1,0:T(8,128)S(1)}, f32[1,2,32,32]{3,2,1,0:T(8,128)}, u32[]{:S(2)}) copy-start(f32[1,2,32,32]{3,2,1,0:T(8,128)} %get-tuple-element.83) | copy-start | bytes 24580
  540.7 41.4 %slice-start = ((s8[16777216]{0:T(1024)(128)(4,1)}), s8[4194304]{0:T(1024)(128)(4,1)S(1)}, s32[]{:S(2)}) async-start(s8[16777216]{0:T(1024)(128)(4,1)} %bitcast.216), calls=%async_computation.3 | async-start | bytes 8388608
  540.7 41.4 %slice-start.1 = ((s8[16777216]{0:T(1024)(128)(4,1)}), s8[4194304]{0:T(1024)(128)(4,1)S(1)}, s32[]{:S(2)}) async-start(s8[16777216]{0:T(1024)(128)(4,1)} %bitcast.216), calls=%async_computation.4 | async-start | bytes 8388608
  559.1 23.0 %slice-start.2 = ((s8[16777216]{0:T(1024)(128)(4,1)}), s8[4194304]{0:T(1024)(128)(4,1)S(1)}, s32[]{:S(2)}) async-start(s8[16777216]{0:T(1024)(128)(4,1)} %bitcast.216), calls=%async_computation.5 | async-start | bytes 8388608
  559.1 23.0 %slice-start.3 = ((s8[16777216]{0:T(1024)(128)(4,1)}), s8[4194304]{0:T(1024)(128)(4,1)S(1)}, s32[]{:S(2)}) async-start(s8[16777216]{0:T(1024)(128)(4,1)} %bitcast.216), calls=%async_computation.6 | async-start | bytes 8388608
  667.4 5.1 copy-start.3
  667.4 5.1 copy-start.4
  672.5 6.0 copy-start.1
Sparse Core Ops, SparseCore 0:
  434.9 232.4 all-reduce.2
where the time goes:
time: 697 us; the launch traced here: 685 us
  local copies, waits for them, and re-layouts  357 us (51%)
  waiting for transfers between devices  136 us (20%)
  matrix products  109 us (16%)
  other arithmetic  53.4 us (8%)
  starting transfers between devices  14.8 us (2%)
  between operations  14.5 us (2%)
    gather x96, local copies, waits for them, and re-layouts  144 us
    psum x1, waiting for transfers between devices, local(): lax.psum((num_real, num_imag, local_weight), ('slab', 'tomo'))  82.8 us
    dot_general x2, matrix products, transform_complex(): state = jnp.einsum(einsum_form, table, state, precision=lax.Precision.HIGH)  36.8 us
    dot_general x2, matrix products, transform_real(): state = jnp.einsum(einsum_form, table, state, precision=lax.Precision.HIGH)  34.6 us
    all_to_all x1, waiting for transfers between devices, local(): lax.all_to_all(slot_labels, 'slab', split_axis=0, concat_axis=0, tiled=True)  32 us
    another operation x2, local copies, waits for them, and re-layouts, local(): jnp.stack((num_real, num_imag), axis=1)  27.5 us
    all_to_all x1, waiting for transfers between devices, local(): lax.all_to_all(outgoing, 'slab', split_axis=0, concat_axis=0, tiled=True)  21.3 us
    dot_general x1, local copies, waits for them, and re-layouts, block_step(): jnp.einsum('sr,sabc->rabc', members, spec_imag, precision=lax.Precision.H...  19.9 us
  transfers between devices with their start and end apart: 5, of which 3 were waited for; matrix products, arithmetic and copies ran while one was open for 24% of the time, Pallas kernels for 0%

commit v1 on v0

v1 whole, which is shorter than its diff:
```python
import functools
import math

import jax
import jax.numpy as jnp
import ml_dtypes
import numpy as np
from jax import lax
from jax.experimental import pallas as pl
from jax.experimental.pallas import tpu as pltpu
from jax.sharding import PartitionSpec as P

GROUP = 8
LIMIT = 56 * 1024 * 1024


def split_table(table):
    high = table.astype(ml_dtypes.bfloat16)
    low = (table - high.astype(np.float64)).astype(ml_dtypes.bfloat16)
    return high, low


def plane_tables(length):
    n = np.arange(length)
    angles = 2.0 * math.pi / length * (np.outer(n, n) % length)
    one = (np.cos(angles) - 1j * np.sin(angles)) / math.sqrt(length)
    both = np.kron(one, one)
    table = np.concatenate((both.real, both.imag), axis=1)
    return np.stack(split_table(table))


def depth_tables(length):
    n = np.arange(length)
    angles = 2.0 * math.pi / length * (np.outer(n, n) % length)
    c = np.cos(angles) / math.sqrt(length)
    s = np.sin(angles) / math.sqrt(length)
    result = []
    for sign in (1.0, -1.0):
        high, low = split_table(np.block([[c, sign * s], [-sign * s, c]]))
        result.append(np.concatenate((high, high, low), axis=1))
    return np.stack(result)


def split(x):
    high = x.astype(jnp.bfloat16)
    return high, (x - high.astype(jnp.float32)).astype(jnp.bfloat16)


def dot(a, b):
    return jnp.dot(a, b, preferred_element_type=jnp.float32)


def depth_pass(table, x):
    high, low = split(x)
    return dot(table, jnp.concatenate((high, low, high), axis=0))


def cut_kernel(info, below, here, above, boxes, sums, volume, window, sems):
    depth, rows, cols = here.shape
    slots, box_len, _ = boxes.shape
    span = box_len + 16
    half = below.shape[0]
    copies = [
        pltpu.make_async_copy(below, volume.at[pl.ds(0, half)], sems.at[0]),
        pltpu.make_async_copy(here, volume.at[pl.ds(half, depth)], sems.at[1]),
        pltpu.make_async_copy(above, volume.at[pl.ds(half + depth, half)], sems.at[2]),
    ]
    for copy in copies:
        copy.start()
    sums[...] = jnp.zeros_like(sums)
    for copy in copies:
        copy.wait()
    lane = lax.broadcasted_iota(jnp.int32, (cols, 128), 1)
    source = lax.broadcasted_iota(jnp.int32, (cols, 128), 0)
    quarter = lax.broadcasted_iota(jnp.int32, (box_len, 128), 1) // box_len

    @pl.loop(0, slots)
    def _(i):
        z0 = info[0, i]
        x0 = info[1, i]
        y0 = info[2, i]
        rot = info[3, i]
        live = info[4, i]
        start = pl.multiple_of(jnp.minimum(x0 // 16 * 16, rows - span), 16)
        pick = (source == y0 + lane % box_len).astype(jnp.float32).astype(jnp.bfloat16)
        cells = volume[pl.ds(z0, box_len), pl.ds(start, span), :]
        window[...] = dot(cells.reshape(box_len * span, cols), pick)
        shift = x0 - start
        for q in range(box_len * box_len // 128):
            part = jnp.zeros((box_len, 128), jnp.float32)
            for e in range(128 // box_len):
                got = window[pl.ds(shift + q * (128 // box_len) + e, box_len, stride=span), :]
                part = jnp.where(quarter == e, got, part)
            lanes = pl.ds(q * 128, 128)
            boxes[i, :, lanes] = part.astype(jnp.bfloat16)

            @pl.when(live > 0)
            def _():
                sums[rot, :, lanes] += part


def score_kernel(rot, boxes, refs, ctf, plane, depth, out, spec, back_high, back_low):
    slots, box_len, cells = boxes.shape
    rows = GROUP * box_len

    @pl.loop(0, slots // GROUP)
    def _(g):
        b = boxes[pl.ds(g * GROUP, GROUP)].reshape(rows, cells)
        spec[...] = (dot(b, plane[0]) + dot(b, plane[1])).reshape(GROUP, box_len, 2 * cells)

        powers = []
        for j in range(GROUP):
            slot = g * GROUP + j
            ref_at = rot[slot]
            x = spec[j]
            x = jnp.concatenate((x[:, :cells], x[:, cells:]), axis=0)
            x = depth_pass(depth[0], x)
            weights = ctf[...]
            sr = x[:box_len] * weights
            si = x[box_len:] * weights
            rr = refs[ref_at, 0]
            ri = refs[ref_at, 1]
            own = jnp.sum(sr * sr + si * si, axis=(0, 1), keepdims=True)
            ref = jnp.sum(rr * rr + ri * ri, axis=(0, 1), keepdims=True)
            powers.append(own * ref)
            prod = jnp.concatenate((sr * rr + si * ri, si * rr - sr * ri), axis=0)
            high, low = split(depth_pass(depth[1], prod))
            at = pl.ds(j * box_len, box_len)
            back_high[at, :cells] = high[:box_len]
            back_high[at, cells:] = high[box_len:]
            back_low[at, :cells] = low[:box_len]
            back_low[at, cells:] = low[box_len:]

        cross = jnp.zeros((rows, cells), jnp.float32)
        for c in range(2):
            lanes = pl.ds(c * cells, cells)
            high = back_high[:, lanes]
            cross += dot(high, plane[0, :, lanes]) + dot(high, plane[1, :, lanes])
            cross += dot(back_low[:, lanes], plane[0, :, lanes])
        for j in range(GROUP):
            part = cross[j * box_len : (j + 1) * box_len]
            peak = jnp.max(part, axis=(0, 1), keepdims=True)
            score = (cells * box_len) * peak / jnp.sqrt(powers[j] + 1e-06)
            out[pl.ds(g * GROUP + j, 1), :] = jnp.broadcast_to(score, (1, 128))


def class_kernel(sums, ctf, plane, depth, out):
    count, box_len, cells = sums.shape
    high, low = split(sums[...].reshape(count * box_len, cells))
    x = dot(high, plane[0]) + dot(high, plane[1]) + dot(low, plane[0])
    for r in range(count):
        part = x[r * box_len : (r + 1) * box_len]
        part = jnp.concatenate((part[:, :cells], part[:, cells:]), axis=0)
        part = depth_pass(depth[0], part)
        at = pl.ds(r * box_len, box_len)
        out[0, at, :] = part[:box_len] * ctf[...]
        out[1, at, :] = part[box_len:] * ctf[...]


VMEM = pl.BlockSpec(memory_space=pltpu.VMEM)
SMEM = pl.BlockSpec(memory_space=pltpu.SMEM)
ANY = pl.BlockSpec(memory_space=pl.ANY)


def local(tomogram, centers, owner, rotation, ctf, ref_spectra, plane, depth):
    slab_count = lax.axis_size("slab")
    tomo_count = lax.axis_size("tomo")
    me = lax.axis_index("slab")
    ref_count, _, box_len, cells = ref_spectra.shape
    half = box_len // 2
    here = tomogram[0]
    slab_depth, rows, cols = here.shape
    slots = owner.shape[1]
    aligned = 16

    n = slab_count
    below = lax.ppermute(here[slab_depth - half :], "slab", [(i, i + 1) for i in range(n - 1)])
    above = lax.ppermute(here[:half], "slab", [(i + 1, i) for i in range(n - 1)])

    labels = jnp.stack((owner[0], rotation[0]))
    all_labels = lax.all_gather(labels, ("tomo", "slab"))
    all_labels = all_labels.reshape(tomo_count, slab_count, 2, slots)
    all_owner = all_labels[:, :, 0].reshape(tomo_count, slab_count * slots)
    all_rotation = all_labels[:, :, 1].reshape(tomo_count, slab_count * slots)
    all_ctf = lax.all_gather(ctf[0], "tomo")

    info = jnp.stack(
        (
            centers[0, 0] - me * slab_depth,
            centers[0, 1] - half,
            centers[0, 2] - half,
            rotation[0],
            (owner[0] >= 0).astype(jnp.int32),
        )
    )
    boxes, sums = pl.pallas_call(
        cut_kernel,
        out_shape=(
            jax.ShapeDtypeStruct((slots, box_len, cells), jnp.bfloat16),
            jax.ShapeDtypeStruct((ref_count, box_len, cells), jnp.float32),
        ),
        in_specs=[SMEM, ANY, ANY, ANY],
        out_specs=(VMEM, VMEM),
        scratch_shapes=[
            pltpu.VMEM((2 * half + slab_depth, rows, cols), jnp.bfloat16),
            pltpu.VMEM((box_len * (box_len + 16), 128), jnp.float32),
            pltpu.SemaphoreType.DMA((3,)),
        ],
        compiler_params=pltpu.CompilerParams(vmem_limit_bytes=LIMIT),
    )(info, below, here, above)

    mine = lax.psum_scatter(sums, "slab", scatter_dimension=0, tiled=True)

    scores = pl.pallas_call(
        score_kernel,
        out_shape=jax.ShapeDtypeStruct((slots, 128), jnp.float32),
        in_specs=[SMEM, VMEM, VMEM, VMEM, VMEM, VMEM],
        out_specs=VMEM,
        scratch_shapes=[
            pltpu.VMEM((GROUP, box_len, 2 * cells), jnp.float32),
            pltpu.VMEM((GROUP * box_len, 2 * cells), jnp.bfloat16),
            pltpu.VMEM((GROUP * box_len, 2 * cells), jnp.bfloat16),
        ],
        compiler_params=pltpu.CompilerParams(vmem_limit_bytes=LIMIT),
        cost_estimate=pl.CostEstimate(
            flops=2 * slots * box_len * cells * 2 * cells * 6, bytes_accessed=20 << 20, transcendentals=0
        ),
    )(rotation[0], boxes, ref_spectra, ctf[0], plane, depth)[:, 0]

    count = ref_count // slab_count
    spectra = pl.pallas_call(
        class_kernel,
        out_shape=jax.ShapeDtypeStruct((2, count * box_len, cells), jnp.float32),
        in_specs=[VMEM] * 4,
        out_specs=VMEM,
        compiler_params=pltpu.CompilerParams(vmem_limit_bytes=LIMIT),
        cost_estimate=pl.CostEstimate(
            flops=2 * count * box_len * cells * 2 * cells * 4, bytes_accessed=10 << 20, transcendentals=0
        ),
    )(mine, ctf[0], plane, depth)
    numer = lax.psum_scatter(spectra, "tomo", scatter_dimension=1, tiled=True)

    per = count * box_len // tomo_count
    first = lax.axis_index("tomo") * per
    r_at = me * count + first // box_len
    hits = (all_rotation == r_at) & (all_owner >= 0)
    times = jnp.sum(hits.astype(jnp.float32), axis=1)
    part_ctf = lax.dynamic_slice_in_dim(all_ctf, first % box_len, per, axis=1)
    weight = jnp.sum(times[:, None, None] * part_ctf * part_ctf, axis=0)
    result = numer / (weight + 1.0)

    largest = jnp.max(jnp.abs(result), axis=2, keepdims=True)
    scale = jnp.where(largest > 0, largest, 1.0) * (1.0 / 32767.0)
    coded = jnp.round(result / scale).astype(jnp.int16)
    coded = lax.all_gather(coded, ("slab", "tomo"))
    scale = lax.all_gather(scale[:, :, 0], ("slab", "tomo"))
    decoded = coded.astype(jnp.float32) * scale[:, :, :, None]
    decoded = decoded.reshape(ref_count, box_len // per, 2, per, cells)
    new_reference = jnp.swapaxes(decoded, 1, 2).reshape(ref_count, 2, box_len, cells)

    all_scores = lax.all_gather(scores, "slab").reshape(slab_count * slots)
    own = lax.dynamic_index_in_dim(all_owner, lax.axis_index("tomo"), 0, keepdims=False) == me
    rank = jnp.cumsum(own.astype(jnp.int32)) - 1
    chosen = own[None, :] & (rank[None, :] == jnp.arange(aligned, dtype=jnp.int32)[:, None])
    score = jnp.sum(jnp.where(chosen, all_scores[None, :], 0.0), axis=1)
    return score.reshape(1, aligned), new_reference


def solution(mesh):
    inner = jax.shard_map(
        local,
        mesh=mesh,
        in_specs=(
            P("tomo", "slab", None, None),
            P("tomo", None, "slab"),
            P("tomo", "slab"),
            P("tomo", "slab"),
            P("tomo", None, None),
            P(),
            P(),
            P(),
        ),
        out_specs=(P("tomo", "slab"), P()),
        check_vma=False,
    )

    def program(tomogram, centers, owner, rotation, ctf, ref_spectra):
        box_len = ref_spectra.shape[2]
        plane = jnp.asarray(plane_tables(box_len))
        depth = jnp.asarray(depth_tables(box_len))
        return inner(tomogram, centers, owner, rotation, ctf, ref_spectra, plane, depth)

    return program
```

time: 697 us -> 400 us (0.57)
  local copies, waits for them, and re-layouts: 357 us -> 3.23 us
  blocking collectives: 0 us -> 290 us
  waiting for transfers between devices: 136 us -> 2.51 us
  matrix products: 109 us -> 0 us
  Pallas kernels: 0 us -> 69.7 us
  other arithmetic: 53.4 us -> 9.6 us
  starting transfers between devices: 14.8 us -> 4.09 us
    all_gather x0 -> x4, blocking collectives: none -> 276 us  [the longest x1 123 us: local(): coded = lax.all_gather(coded, ('slab', 'tomo'))]
    gather x103 -> x0, local copies, waits for them, and re-layouts: 182 us -> none
    dot_general x8 -> x0, matrix products: 109 us -> none  [the longest x2 36.8 us: transform_complex(): state = jnp.einsum(einsum_form, table, state, precision=lax.Precision.HIGH)]
    psum x1 -> x0, waiting for transfers between devices: 82.8 us -> none  [local(): lax.psum((num_real, num_imag, local_weight), ('slab', 'tomo'))]
    another operation x8 -> x3, local copies, waits for them, and re-layouts: 71.7 us -> 1.46 us  [the longest x1 1.26 us: local(): jnp.stack((centers[0, 0] - me * slab_depth, centers[0, 1] - half, centers...]
    pallas_call x0 -> x3, Pallas kernels: none -> 69.7 us  [the longest x1 38.9 us: local(): pl.pallas_call(score_kernel, out_shape=jax.ShapeDtypeStruct((slots, 128),...]
    all_to_all x2 -> x0, waiting for transfers between devices: 53.2 us -> none  [the longest x1 32 us: local(): lax.all_to_all(slot_labels, 'slab', split_axis=0, concat_axis=0, tiled=True)]
    reshape x4 -> x0, local copies, waits for them, and re-layouts: 43.5 us -> none  [the longest x1 12.4 us: local(): boxes[slot_table].reshape(slab_count, capacity, box_len, box_len * box_len)]
  transfers between devices with their start and end apart: 5 -> 4, of which waited for: 3 -> 1; matrix products, arithmetic and copies ran while one was open for 24% -> 1% of each run, Pallas kernels for 0% -> 10%
where the time goes in v1:
time: 400 us; the launch traced here: 394 us
  blocking collectives  290 us (72%)
  Pallas kernels  69.7 us (17%)
  between operations  14.8 us (4%)
  other arithmetic  9.6 us (2%)
  starting transfers between devices  4.09 us (1%)
    all_gather x1, blocking collectives, local(): coded = lax.all_gather(coded, ('slab', 'tomo'))  123 us
    all_gather x1, blocking collectives, local(): all_labels = lax.all_gather(labels, ('tomo', 'slab'))  69.9 us
    all_gather x1, blocking collectives, local(): scale = lax.all_gather(scale[:, :, 0], ('slab', 'tomo'))  61.8 us
    pallas_call x1, Pallas kernels, local(): pl.pallas_call(score_kernel, out_shape=jax.ShapeDtypeStruct((slots, 128),...  38.9 us
    pallas_call x1, Pallas kernels, local(): pl.pallas_call(cut_kernel, out_shape=(jax.ShapeDtypeStruct((slots, box_le...  24 us
    all_gather x1, blocking collectives, local(): all_ctf = lax.all_gather(ctf[0], 'tomo')  20.9 us
    unnamed x1, blocking collectives  14.4 us
  transfers between devices with their start and end apart: 4, of which 1 were waited for; matrix products, arithmetic and copies ran while one was open for 1% of the time, Pallas kernels for 10%

profile of v1, /device:TPU:15, one launch (start us, length us, event | category | flops | bytes accessed | tf_op | source)
XLA Modules:
  0.0 394.0 jit_solution(4185402733128422804)
XLA Ops:
  7.2 0.0 reduce-scatter.3.cloned.1.call-start
  7.2 2.7 collective-permute-start.1
  9.9 1.3 collective-permute-start
  11.2 0.7 compare_convert_fusion.1
  11.9 0.7 add_bitcast_fusion.2
  12.6 1.3 stack.5.info
  13.9 2.4 collective-permute-done.below
  16.3 24.0 %shard_map.95 = (bf16[32,32,1024]{2,1,0:T(8,128)(2,1)}, f32[32,32,1024]{2,1,0:T(8,128)}) custom-call(s32[5,32]{1,0:T(8,128)} %stack.5.info, bf16[16,256,256]{2,1,0:T(8,128)(2,1)} %collective-permute-done.below, bf16[16,256,256]{2,1,0:T(8,128)(2,1)} %bitcast.30, bf16[16,256,256]{2,1,0:T(8,128)(2,1)} %copy-done), custom_call_target="tpu_custom_call" | custom-call | tf_op jit(solution)/shard_map/pallas_call | solution.py:196
  40.3 0.0 reduce-scatter.3.cloned.1.call-update
  40.4 0.0 reduce-scatter.5.cloned.1.call-start
  40.5 69.9 %all-gather.3 = s32[32,2,32]{2,1,0:T(2,128)S(1)} all-gather(s32[1,2,32]{2,1,0:T(2,128)S(1)} %add_bitcast_fusion), channel_id=2, replica_groups=mesh['slab'=8,'tomo'=4] {'tomo','slab'}, dimensions={0}, use_global_device_ids=true | all-gather | bytes 8448 | tf_op jit(solution)/shard_map/all_gather | solution.py:181
  110.4 0.1 reshape_squeeze.4
  110.5 0.3 reduce-window.9
  110.8 0.1 slice.26
  111.0 0.6 dynamic-slice
  112.2 0.1 slice_reduce_fusion.1
  112.3 0.1 convert_reduce_fusion
  112.4 20.9 %all_gather.24 = f32[4,32,1024]{2,1,0:T(8,128)S(1)} all-gather(f32[1,32,1024]{2,1,0:T(8,128)S(1)} %copy-done.1), channel_id=1, replica_groups=mesh['slab'=8,'tomo'=4] {'tomo'}, dimensions={0}, use_global_device_ids=true | all-gather | bytes 655360 | tf_op jit(solution)/shard_map/all_gather | solution.py:185
  133.3 0.1 fusion
  133.4 0.1 add_bitcast_fusion.1
  133.5 0.0 reduce-scatter.3.cloned.1.call-done.sums
  133.5 6.7 %shard_map.97 = f32[2,128,1024]{2,1,0:T(8,128)} custom-call(f32[4,32,1024]{2,1,0:T(8,128)} %reduce-scatter.3.cloned.1.call-done.sums, f32[32,1024]{1,0:T(8,128)} %bitcast.31, bf16[2,1024,2048]{2,1,0:T(8,128)(2,1)} %constant.65.clone.plane, bf16[2,64,192]{2,1,0:T(8,128)(2,1)} %constant.66.clone.depth), custom_call_target="tpu_custom_call" | custom-call | flops 2147483648 | bytes 10485760 | tf_op jit(solution)/shard_map/pallas_call | solution.py:231
  140.3 38.9 %shard_map.96 = f32[32,128]{1,0:T(8,128)} custom-call(s32[32]{0:T(128)} %bitcast.38, bf16[32,32,1024]{2,1,0:T(8,128)(2,1)} %get-tuple-element.4.boxes, f32[32,2,32,1024]{3,2,1,0:T(8,128)} %refs.1, f32[32,1024]{1,0:T(8,128)} %bitcast.32, bf16[2,1024,2048]{2,1,0:T(8,128)(2,1)} %constant.65.clone.plane, bf16[2,64,192]{2,1,0:T(8,128)(2,1)} %constant.66.clone.depth), custom_call_target="tpu_custom_call" | custom-call | flops 25769803776 | bytes 20971520 | tf_op jit(solution)/shard_map/pallas_call | solution.py:214
  179.2 0.8 slice_reduce_fusion
  180.1 0.2 dynamic-update-slice
  180.3 14.4 %all-reduce = f32[256]{0:T(256)S(1)} all-reduce(f32[256]{0:T(256)S(1)} %dynamic-update-slice), channel_id=3, replica_groups=mesh['slab'=8,'tomo'=4] {'slab'}, use_global_device_ids=true, to_apply=%add | all-reduce | flops 256 | bytes 2048
  194.7 0.6 select_reduce_fusion
  195.4 1.0 abs_reduce_fusion
  196.4 61.8 %all_gather.27 = f32[32,2,32]{2,1,0:T(2,128)S(1)} all-gather(f32[1,2,32]{2,1,0:T(2,128)S(1)} %fusion.3), channel_id=1, replica_groups=mesh['slab'=8,'tomo'=4] {'slab','tomo'}, dimensions={0}, use_global_device_ids=true | all-gather | bytes 8448 | tf_op jit(solution)/shard_map/all_gather | solution.py:256
  258.2 1.1 round-nearest-even_convert_fusion
  259.3 123.0 %all-gather.5 = s16[64,32,1024]{2,1,0:T(8,128)(2,1)S(1)} all-gather(s16[2,32,1024]{2,1,0:T(8,128)(2,1)S(1)} %round-nearest-even_convert_fusion), channel_id=4, replica_groups=mesh['slab'=8,'tomo'=4] {'slab','tomo'}, dimensions={0}, use_global_device_ids=true | all-gather | bytes 4325376 | tf_op jit(solution)/shard_map/all_gather | solution.py:255
  382.4 4.8 %convert_multiply_fusion = f32[32,2,32,1024]{3,2,1,0:T(8,128)} fusion(s16[32,2,32,1024]{3,2,1,0:T(8,128)(2,1)S(1)} %bitcast.27, f32[32,2,32]{2,1,0:T(2,128)S(1)} %all_gather.27), kind=kLoop, calls=%fused_computation | loop fusion | flops 4194304 | bytes 12591104 | tf_op jit(solution)/shard_map/mul | solution.py:257
  (21 shorter events, 0.2 us)
Async XLA Ops:
  7.2 126.4 %reduce-scatter.3.cloned.1.call-start = ((), (), s32[]{:S(2)}) async-start(), calls=%async_computation.2 | async-start | bytes 4718592 | tf_op jit(solution)/shard_map/reduce_scatter | solution.py:212
  7.2 6.7 %collective-permute-start.1 = (bf16[16,256,256]{2,1,0:T(8,128)(2,1)}, bf16[16,256,256]{2,1,0:T(8,128)(2,1)S(1)}, u32[]{:S(2)}, u32[]{:S(2)}) collective-permute-start(bf16[16,256,256]{2,1,0:T(8,128)(2,1)} %bitcast.28), channel_id=1, source_target_pairs={{4,0},{8,4},{12,8},{16,12},{20,16},{24,20},{28,24},{5,1},{9,5},{13... | collective-permute-start | bytes 6291464 | tf_op jit(solution)/shard_map/ppermute | solution.py:178
  9.9 6.4 %collective-permute-start = (bf16[16,256,256]{2,1,0:T(8,128)(2,1)}, bf16[16,256,256]{2,1,0:T(8,128)(2,1)}, u32[]{:S(2)}, u32[]{:S(2)}) collective-permute-start(bf16[16,256,256]{2,1,0:T(8,128)(2,1)} %bitcast.29), channel_id=1, source_target_pairs={{0,4},{4,8},{8,12},{12,16},{16,20},{20,24},{24,28},{1,5},{5,9},{9,... | collective-permute-start | bytes 6291464 | tf_op jit(solution)/shard_map/ppermute | solution.py:177
  13.9 26.6 %copy-start.2 = (s32[1,32]{1,0:T(1,128)S(1)}, s32[1,32]{1,0:T(1,128)}, u32[]{:S(2)}) copy-start(s32[1,32]{1,0:T(1,128)} %param.11) | copy-start | bytes 388
  13.9 26.6 %copy-start.3 = (s32[1,32]{1,0:T(1,128)S(1)}, s32[1,32]{1,0:T(1,128)}, u32[]{:S(2)}) copy-start(s32[1,32]{1,0:T(1,128)} %param.10) | copy-start | bytes 388
  13.9 97.1 %copy-start.4 = (u32[32]{0:T(128)S(1)}, u32[32]{0:T(128)}, u32[]{:S(2)}) copy-start(u32[32]{0:T(128)} %constant.74) | copy-start | bytes 388
  13.9 98.6 %copy-start.1 = (f32[1,32,1024]{2,1,0:T(8,128)S(1)}, f32[1,32,1024]{2,1,0:T(8,128)}, u32[]{:S(2)}) copy-start(f32[1,32,1024]{2,1,0:T(8,128)} %param.12) | copy-start | bytes 393220
  13.9 2.5 copy-start
  40.4 155.0 %reduce-scatter.5.cloned.1.call-start = ((), (), s32[]{:S(2)}) async-start(), calls=%async_computation.3 | async-start | bytes 1310720 | tf_op jit(solution)/shard_map/reduce_scatter | solution.py:241
Sparse Core Ops, SparseCore 0:
  40.5 92.5 reduce-scatter.2
  140.4 29.7 reduce-scatter.4

commit v2 on v1

--- a/solution.py
+++ b/solution.py
@@ -55,21 +55,15 @@
     return dot(table, jnp.concatenate((high, low, high), axis=0))
 
 
-def cut_kernel(info, below, here, above, boxes, sums, volume, window, sems):
+def cut_kernel(info, below, here, above, boxes, sums, volume, window):
     depth, rows, cols = here.shape
     slots, box_len, _ = boxes.shape
     span = box_len + 16
     half = below.shape[0]
-    copies = [
-        pltpu.make_async_copy(below, volume.at[pl.ds(0, half)], sems.at[0]),
-        pltpu.make_async_copy(here, volume.at[pl.ds(half, depth)], sems.at[1]),
-        pltpu.make_async_copy(above, volume.at[pl.ds(half + depth, half)], sems.at[2]),
-    ]
-    for copy in copies:
-        copy.start()
     sums[...] = jnp.zeros_like(sums)
-    for copy in copies:
-        copy.wait()
+    volume[:half] = below[...]
+    volume[half : half + depth] = here[...]
+    volume[half + depth :] = above[...]
     lane = lax.broadcasted_iota(jnp.int32, (cols, 128), 1)
     source = lax.broadcasted_iota(jnp.int32, (cols, 128), 0)
     quarter = lax.broadcasted_iota(jnp.int32, (box_len, 128), 1) // box_len
@@ -96,7 +90,11 @@
 
             @pl.when(live > 0)
             def _():
-                sums[rot, :, lanes] += part
+                sums[rot, :box_len, lanes] += part
+
+        @pl.when(live > 0)
+        def _():
+            sums[rot, box_len:, :] += 1.0
 
 
 def score_kernel(rot, boxes, refs, ctf, plane, depth, out, spec, back_high, back_low):
@@ -145,8 +143,9 @@
 
 
 def class_kernel(sums, ctf, plane, depth, out):
-    count, box_len, cells = sums.shape
-    high, low = split(sums[...].reshape(count * box_len, cells))
+    count = sums.shape[0]
+    box_len, cells = ctf.shape
+    high, low = split(sums[:, :box_len, :].reshape(count * box_len, cells))
     x = dot(high, plane[0]) + dot(high, plane[1]) + dot(low, plane[0])
     for r in range(count):
         part = x[r * box_len : (r + 1) * box_len]
@@ -155,6 +154,96 @@
         at = pl.ds(r * box_len, box_len)
         out[0, at, :] = part[:box_len] * ctf[...]
         out[1, at, :] = part[box_len:] * ctf[...]
+        out[2, at, :] = sums[r, box_len : box_len + 1, :] * ctf[...] * ctf[...]
+
+
+def gather_kernel(slabs, tomos, chunk, labels, out, tags, send, arrive, tag_send, tag_arrive, local_sems):
+    s = lax.axis_index("slab")
+    t = lax.axis_index("tomo")
+    pairs = slabs // 2
+    parity = lax.rem(s, 2)
+    pair = s // 2
+    sibling = s + 1 - 2 * parity
+    peers = [lax.rem(pair + d, pairs) * 2 + parity for d in range(1, pairs)]
+    depths = [lax.rem(t + d, tomos) for d in range(1, tomos)]
+    mates = [lax.rem(s + d, slabs) for d in range(1, slabs)]
+
+    barrier = pltpu.get_barrier_semaphore()
+    partners = [(s, d) for d in depths] + [(m, t) for m in mates]
+    for place in partners:
+        pl.semaphore_signal(barrier, inc=1, device_id=place, device_id_type=pl.DeviceIdType.MESH)
+    pl.semaphore_wait(barrier, len(partners))
+
+    started = []
+
+    def push(source, at_s, at_t, place):
+        copy = pltpu.make_async_remote_copy(
+            src_ref=source,
+            dst_ref=out.at[at_s, at_t],
+            send_sem=send.at[len(started)],
+            recv_sem=arrive.at[at_s, at_t],
+            device_id=place,
+            device_id_type=pl.DeviceIdType.MESH,
+        )
+        copy.start()
+        started.append(copy)
+
+    def landed(at_s, at_t):
+        pltpu.make_async_remote_copy(
+            src_ref=out.at[at_s, at_t],
+            dst_ref=out.at[at_s, at_t],
+            send_sem=send.at[0],
+            recv_sem=arrive.at[at_s, at_t],
+            device_id=(sibling, t),
+            device_id_type=pl.DeviceIdType.MESH,
+        ).wait_recv()
+
+    own = pltpu.make_async_copy(chunk, out.at[s, t], local_sems.at[0])
+    own.start()
+    own_tag = pltpu.make_async_copy(labels, tags.at[s], local_sems.at[1])
+    own_tag.start()
+    for d in depths:
+        push(chunk, s, t, (s, d))
+    for p in peers:
+        push(chunk, s, t, (p, t))
+    push(chunk, s, t, (sibling, t))
+    tag_copies = []
+    for i, m in enumerate(mates):
+        copy = pltpu.make_async_remote_copy(
+            src_ref=labels,
+            dst_ref=tags.at[s],
+            send_sem=tag_send.at[i],
+            recv_sem=tag_arrive.at[s],
+            device_id=(m, t),
+            device_id_type=pl.DeviceIdType.MESH,
+        )
+        copy.start()
+        tag_copies.append(copy)
+    for d in depths:
+        landed(s, d)
+        for p in peers:
+            push(out.at[s, d], s, d, (p, t))
+        push(out.at[s, d], s, d, (sibling, t))
+    for d in [t] + depths:
+        for p in peers:
+            landed(p, d)
+            push(out.at[p, d], p, d, (sibling, t))
+    for d in [t] + depths:
+        for p in [pair * 2 + 1 - parity] + [q + 1 - 2 * parity for q in peers]:
+            landed(p, d)
+    for m in mates:
+        pltpu.make_async_remote_copy(
+            src_ref=labels,
+            dst_ref=tags.at[m],
+            send_sem=tag_send.at[0],
+            recv_sem=tag_arrive.at[m],
+            device_id=(m, t),
+            device_id_type=pl.DeviceIdType.MESH,
+        ).wait_recv()
+    own.wait()
+    own_tag.wait()
+    for copy in started + tag_copies:
+        copy.wait_send()
 
 
 VMEM = pl.BlockSpec(memory_space=pltpu.VMEM)
@@ -176,13 +265,6 @@
     n = slab_count
     below = lax.ppermute(here[slab_depth - half :], "slab", [(i, i + 1) for i in range(n - 1)])
     above = lax.ppermute(here[:half], "slab", [(i + 1, i) for i in range(n - 1)])
-
-    labels = jnp.stack((owner[0], rotation[0]))
-    all_labels = lax.all_gather(labels, ("tomo", "slab"))
-    all_labels = all_labels.reshape(tomo_count, slab_count, 2, slots)
-    all_owner = all_labels[:, :, 0].reshape(tomo_count, slab_count * slots)
-    all_rotation = all_labels[:, :, 1].reshape(tomo_count, slab_count * slots)
-    all_ctf = lax.all_gather(ctf[0], "tomo")
 
     info = jnp.stack(
         (
@@ -197,23 +279,22 @@
         cut_kernel,
         out_shape=(
             jax.ShapeDtypeStruct((slots, box_len, cells), jnp.bfloat16),
-            jax.ShapeDtypeStruct((ref_count, box_len, cells), jnp.float32),
-        ),
-        in_specs=[SMEM, ANY, ANY, ANY],
+            jax.ShapeDtypeStruct((ref_count, box_len + 8, cells), jnp.float32),
+        ),
+        in_specs=[SMEM, VMEM, VMEM, VMEM],
         out_specs=(VMEM, VMEM),
         scratch_shapes=[
             pltpu.VMEM((2 * half + slab_depth, rows, cols), jnp.bfloat16),
             pltpu.VMEM((box_len * (box_len + 16), 128), jnp.float32),
-            pltpu.SemaphoreType.DMA((3,)),
         ],
         compiler_params=pltpu.CompilerParams(vmem_limit_bytes=LIMIT),
     )(info, below, here, above)
 
     mine = lax.psum_scatter(sums, "slab", scatter_dimension=0, tiled=True)
 
-    scores = pl.pallas_call(
+    score_call = lambda part: pl.pallas_call(
         score_kernel,
-        out_shape=jax.ShapeDtypeStruct((slots, 128), jnp.float32),
+        out_shape=jax.ShapeDtypeStruct((part, 128), jnp.float32),
         in_specs=[SMEM, VMEM, VMEM, VMEM, VMEM, VMEM],
         out_specs=VMEM,
         scratch_shapes=[
@@ -223,14 +304,22 @@
         ],
         compiler_params=pltpu.CompilerParams(vmem_limit_bytes=LIMIT),
         cost_estimate=pl.CostEstimate(
-            flops=2 * slots * box_len * cells * 2 * cells * 6, bytes_accessed=20 << 20, transcendentals=0
-        ),
-    )(rotation[0], boxes, ref_spectra, ctf[0], plane, depth)[:, 0]
+            flops=2 * part * box_len * cells * 2 * cells * 8, bytes_accessed=20 << 20, transcendentals=0
+        ),
+    )
+    def score_part(i, length):
+        return score_call(length)(
+            rotation[0, i : i + length], boxes[i : i + length], ref_spectra, ctf[0], plane, depth
+        )[:, 0]
+
+    part = slots * 3 // 4
+    early = score_part(0, part)
+    mine, early = lax.optimization_barrier((mine, early))
 
     count = ref_count // slab_count
     spectra = pl.pallas_call(
         class_kernel,
-        out_shape=jax.ShapeDtypeStruct((2, count * box_len, cells), jnp.float32),
+        out_shape=jax.ShapeDtypeStruct((3, count * box_len, cells), jnp.float32),
         in_specs=[VMEM] * 4,
         out_specs=VMEM,
         compiler_params=pltpu.CompilerParams(vmem_limit_bytes=LIMIT),
@@ -239,27 +328,53 @@
         ),
     )(mine, ctf[0], plane, depth)
     numer = lax.psum_scatter(spectra, "tomo", scatter_dimension=1, tiled=True)
+    scores = jnp.concatenate((early, score_part(part, slots - part)))
 
     per = count * box_len // tomo_count
-    first = lax.axis_index("tomo") * per
-    r_at = me * count + first // box_len
-    hits = (all_rotation == r_at) & (all_owner >= 0)
-    times = jnp.sum(hits.astype(jnp.float32), axis=1)
-    part_ctf = lax.dynamic_slice_in_dim(all_ctf, first % box_len, per, axis=1)
-    weight = jnp.sum(times[:, None, None] * part_ctf * part_ctf, axis=0)
-    result = numer / (weight + 1.0)
+    result = numer[:2] / (numer[2:] + 1.0)
 
     largest = jnp.max(jnp.abs(result), axis=2, keepdims=True)
-    scale = jnp.where(largest > 0, largest, 1.0) * (1.0 / 32767.0)
-    coded = jnp.round(result / scale).astype(jnp.int16)
-    coded = lax.all_gather(coded, ("slab", "tomo"))
-    scale = lax.all_gather(scale[:, :, 0], ("slab", "tomo"))
-    decoded = coded.astype(jnp.float32) * scale[:, :, :, None]
-    decoded = decoded.reshape(ref_count, box_len // per, 2, per, cells)
+    power = jnp.floor(jnp.log2(jnp.maximum(largest, 2.0**-90))) - 13.0
+    digits = jnp.ceil(largest / jnp.exp2(power))
+
+    def row_scale(digits, power):
+        return jnp.maximum(digits, 1.0) * jnp.exp2(power) * (1.0 / 32767.0)
+
+    coded = jnp.clip(jnp.round(result / row_scale(digits, power)), -32767.0, 32767.0)
+    lane = lax.broadcasted_iota(jnp.int32, (2, per, 128), 2)
+    coded = jnp.concatenate((coded, jnp.where(lane == 0, digits, power)), axis=2)
+    coded = coded.astype(jnp.int16).reshape(2 * per, cells + 128)
+    labels = jnp.zeros((8, 128), jnp.float32).at[0, :slots].set(scores)
+    labels = labels.at[1, :slots].set(owner[0].astype(jnp.float32))
+    pairs = slab_count // 2
+    sends = tomo_count - 1 + pairs + (tomo_count - 1) * pairs + tomo_count * (pairs - 1)
+    gathered, tags = pl.pallas_call(
+        functools.partial(gather_kernel, slab_count, tomo_count),
+        out_shape=(
+            jax.ShapeDtypeStruct((slab_count, tomo_count, 2 * per, cells + 128), jnp.int16),
+            jax.ShapeDtypeStruct((slab_count, 8, 128), jnp.float32),
+        ),
+        in_specs=[ANY, ANY],
+        out_specs=(ANY, ANY),
+        scratch_shapes=[
+            pltpu.SemaphoreType.DMA((sends,)),
+            pltpu.SemaphoreType.DMA((slab_count, tomo_count)),
+            pltpu.SemaphoreType.DMA((slab_count,)),
+            pltpu.SemaphoreType.DMA((slab_count,)),
+            pltpu.SemaphoreType.DMA((2,)),
+        ],
+        compiler_params=pltpu.CompilerParams(
+            collective_id=0, has_side_effects=True, vmem_limit_bytes=LIMIT
+        ),
+    )(coded, labels)
+    gathered = gathered.reshape(ref_count, box_len // per, 2, per, cells + 128)
+    head = gathered[..., cells : cells + 2].astype(jnp.float32)
+    scale = row_scale(head[..., :1], head[..., 1:])
+    decoded = gathered[..., :cells].astype(jnp.float32) * scale
     new_reference = jnp.swapaxes(decoded, 1, 2).reshape(ref_count, 2, box_len, cells)
 
-    all_scores = lax.all_gather(scores, "slab").reshape(slab_count * slots)
-    own = lax.dynamic_index_in_dim(all_owner, lax.axis_index("tomo"), 0, keepdims=False) == me
+    all_scores = tags[:, 0, :slots].reshape(slab_count * slots)
+    own = tags[:, 1, :slots].reshape(slab_count * slots).astype(jnp.int32) == me
     rank = jnp.cumsum(own.astype(jnp.int32)) - 1
     chosen = own[None, :] & (rank[None, :] == jnp.arange(aligned, dtype=jnp.int32)[:, None])
     score = jnp.sum(jnp.where(chosen, all_scores[None, :], 0.0), axis=1)

time: 400 us -> 245 us (0.61); the launches traced: 394 us -> 245 us
  blocking collectives: 290 us -> 0 us
  waiting for transfers between devices: 2.51 us -> 83.2 us
  Pallas kernels: 69.7 us -> 119 us
  local copies, waits for them, and re-layouts: 3.23 us -> 10.2 us
  other arithmetic: 9.6 us -> 13.7 us
    all_gather x4 -> x0, blocking collectives: 276 us -> none  [the longest x1 123 us: local(): coded = lax.all_gather(coded, ('slab', 'tomo'))]
    reduce_scatter x1, waiting for transfers between devices: 0.02 us -> 63.2 us  [local(): mine = lax.psum_scatter(sums, 'slab', scatter_dimension=0, tiled=True)]
    pallas_call x2 -> x4, Pallas kernels: 45.7 us -> 95.1 us  [the longest x2 45.5 us: score_part(): score_call(length)]
    reduce_scatter x1, waiting for transfers between devices: 0.01 us -> 17.5 us  [local(): numer = lax.psum_scatter(spectra, 'tomo', scatter_dimension=1, tiled=True)]
    unnamed x1 -> x0, blocking collectives: 14.4 us -> none
    another operation x0 -> x1, other arithmetic: none -> 5.69 us  [local(): jnp.swapaxes(decoded, 1, 2).reshape(ref_count, 2, box_len, cells)]
    mul x3 -> x2, other arithmetic: 4.79 us -> 0.05 us  [the longest x1 0.03 us: row_scale(): return jnp.maximum(digits, 1.0) * jnp.exp2(power) * (1.0 / 32767.0)]
    slice x3 -> x6, local copies, waits for them, and re-layouts: 0.93 us -> 5.61 us  [the longest x2 2.16 us: score_part(): boxes[i:i + length]]
  transfers between devices with their start and end apart: 4 -> 4, of which waited for: 1 -> 3; matrix products, arithmetic and copies ran while one was open for 1% -> 3% of each run, Pallas kernels for 10% -> 19%
where the time goes in v2:
time: 245 us
  Pallas kernels  119 us (49%)
  waiting for transfers between devices  83.2 us (34%)
  between operations  14.2 us (6%)
  other arithmetic  13.7 us (6%)
  local copies, waits for them, and re-layouts  10.2 us (4%)
  starting transfers between devices  4.09 us (2%)
    reduce_scatter x1, waiting for transfers between devices, local(): mine = lax.psum_scatter(sums, 'slab', scatter_dimension=0, tiled=True)  63.2 us
    pallas_call x2, Pallas kernels, score_part(): score_call(length)  45.5 us
    pallas_call x1, Pallas kernels, local(): pl.pallas_call(functools.partial(gather_kernel, slab_count, tomo_count),...  42.6 us
    pallas_call x1, Pallas kernels, local(): pl.pallas_call(cut_kernel, out_shape=(jax.ShapeDtypeStruct((slots, box_le...  24.3 us
    reduce_scatter x1, waiting for transfers between devices, local(): numer = lax.psum_scatter(spectra, 'tomo', scatter_dimension=1, tiled=True)  17.5 us
    pallas_call x1, Pallas kernels, local(): pl.pallas_call(class_kernel, out_shape=jax.ShapeDtypeStruct((3, count * b...  6.97 us
    another operation x1, other arithmetic, local(): jnp.swapaxes(decoded, 1, 2).reshape(ref_count, 2, box_len, cells)  5.69 us
  transfers between devices with their start and end apart: 4, of which 3 were waited for; matrix products, arithmetic and copies ran while one was open for 3% of the time, Pallas kernels for 19%

profile of v2, /device:TPU:15, one launch (start us, length us, event | category | flops | bytes accessed | tf_op | source)
XLA Modules:
  0.0 244.7 jit_solution(5872318459110555839)
XLA Ops:
  7.2 2.7 %collective-permute-start.1 = (bf16[16,256,256]{2,1,0:T(8,128)(2,1)}, bf16[16,256,256]{2,1,0:T(8,128)(2,1)S(1)}, u32[]{:S(2)}, u32[]{:S(2)}) collective-permute-start(bf16[16,256,256]{2,1,0:T(8,128)(2,1)} %bitcast.27), channel_id=1, source_target_pairs={{4,0},{8,4},{12,8},{16,12},{20,16},{24,20},{28,24},{5,1},{9,5},{13... | collective-permute-start | bytes 6291464 | tf_op jit(solution)/shard_map/ppermute | solution.py:267
  9.9 1.3 collective-permute-start
  11.2 0.7 compare_convert_fusion.1
  11.9 0.7 add_bitcast_fusion.1
  12.6 1.3 stack.2.info
  13.9 2.5 %collective-permute-done.below = bf16[16,256,256]{2,1,0:T(8,128)(2,1)} collective-permute-done((bf16[16,256,256]{2,1,0:T(8,128)(2,1)}, bf16[16,256,256]{2,1,0:T(8,128)(2,1)}, u32[]{:S(2)}, u32[]{:S(2)}) %collective-permute-start) | collective-permute-done | bytes 2097184 | tf_op jit(solution)/shard_map/ppermute | solution.py:266
  16.3 24.3 %shard_map.95 = (bf16[32,32,1024]{2,1,0:T(8,128)(2,1)}, f32[32,40,1024]{2,1,0:T(8,128)}) custom-call(s32[5,32]{1,0:T(8,128)} %stack.2.info, bf16[16,256,256]{2,1,0:T(8,128)(2,1)} %collective-permute-done.below, bf16[16,256,256]{2,1,0:T(8,128)(2,1)} %bitcast.29, bf16[16,256,256]{2,1,0:T(8,128)(2,1)} %copy-done.1), custom_call_target="tpu_custom_call" | custom-call | tf_op jit(solution)/shard_map/pallas_call | solution.py:278
  40.8 0.5 slice_bitcast_fusion.1.rot
  41.3 1.0 copy-done
  42.3 1.3 slice.97.boxes
  43.6 31.0 %shard_map.96 = f32[24,128]{1,0:T(8,128)} custom-call(s32[24]{0:T(128)} %slice_bitcast_fusion.1.rot, bf16[24,32,1024]{2,1,0:T(8,128)(2,1)} %slice.97.boxes, f32[32,2,32,1024]{3,2,1,0:T(8,128)} %refs.3, f32[32,1024]{1,0:T(8,128)} %bitcast.31, bf16[2,1024,2048]{2,1,0:T(8,128)(2,1)} %constant.104.clone.plane, bf16[2,64,192]{2,1,0:T(8,128)(2,1)} %constant.105.clone.depth), custom_call_target="tpu_custom_call" | custom-call | flops 25769803776 | bytes 20971520 | tf_op jit(solution)/shard_map/pallas_call | solution.py:311
  74.6 0.8 slice_reduce_fusion
  75.4 63.2 %reduce-scatter.3.cloned.1.call-done.sums = f32[4,40,1024]{2,1,0:T(8,128)} async-done(((f32[32,40,1024]{2,1,0:T(8,128)}), f32[4,40,1024]{2,1,0:T(8,128)}) %reduce-scatter.3.cloned.1.call-update) | async-done | bytes 655376 | tf_op jit(solution)/shard_map/reduce_scatter | solution.py:293
  138.6 7.0 %shard_map.97 = f32[3,128,1024]{2,1,0:T(8,128)} custom-call(f32[4,40,1024]{2,1,0:T(8,128)} %reduce-scatter.3.cloned.1.call-done.sums, f32[32,1024]{1,0:T(8,128)} %bitcast.32, bf16[2,1024,2048]{2,1,0:T(8,128)(2,1)} %constant.104.clone.plane, bf16[2,64,192]{2,1,0:T(8,128)(2,1)} %constant.105.clone.depth), custom_call_target="tpu_custom_call" | custom-call | flops 2147483648 | bytes 10485760 | tf_op jit(solution)/shard_map/pallas_call | solution.py:320
  145.7 0.6 slice_bitcast_fusion.rot
  146.2 0.8 slice.102.boxes
  147.1 14.5 %shard_map.98 = f32[8,128]{1,0:T(8,128)} custom-call(s32[8]{0:T(128)} %slice_bitcast_fusion.rot, bf16[8,32,1024]{2,1,0:T(8,128)(2,1)} %slice.102.boxes, f32[32,2,32,1024]{3,2,1,0:T(8,128)} %refs.3, f32[32,1024]{1,0:T(8,128)} %bitcast.33, bf16[2,1024,2048]{2,1,0:T(8,128)(2,1)} %constant.104.clone.plane, bf16[2,64,192]{2,1,0:T(8,128)(2,1)} %constant.105.clone.depth), custom_call_target="tpu_custom_call" | custom-call | flops 8589934592 | bytes 20971520 | tf_op jit(solution)/shard_map/pallas_call | solution.py:311
  161.6 0.8 slice_reduce_fusion.2
  162.6 17.5 %reduce-scatter.5.cloned.1.call-done = f32[3,32,1024]{2,1,0:T(8,128)} async-done(((f32[3,128,1024]{2,1,0:T(8,128)}), f32[3,32,1024]{2,1,0:T(8,128)}) %reduce-scatter.5.cloned.1.call-update) | async-done | bytes 393232 | tf_op jit(solution)/shard_map/reduce_scatter | solution.py:330
  180.1 0.9 fusion
  181.0 1.1 abs_reduce_fusion
  182.3 1.1 clamp_convert_fusion
  183.4 0.7 pad_add_fusion.chunk
  184.1 42.6 %shard_map.99 = (s16[8,4,64,1152]{3,2,1,0:T(8,128)(2,1)}, f32[8,8,128]{2,1,0:T(8,128)}) custom-call(s16[64,1152]{1,0:T(8,128)(2,1)} %pad_add_fusion.chunk, f32[8,128]{1,0:T(8,128)} %copy-done.2), custom_call_target="tpu_custom_call" | custom-call | tf_op jit(solution)/shard_map/pallas_call | solution.py:351
  226.7 0.8 compare_reduce_fusion
  227.5 0.8 fusion.6
  228.3 0.8 slice_reduce_fusion.1
  229.3 0.3 reduce-window.9
  229.9 1.1 slice.116
  231.0 0.5 copy.14
  231.6 5.7 %multiply_bitcast_fusion = f32[32,2,32,1024]{3,2,1,0:T(8,128)} fusion(s16[32,1,2,32,1152]{4,3,2,0,1:T(8,128)(2,1)} %bitcast.26, f32[32,2,32]{2,1,0:T(2,128)S(1)} %copy.13), kind=kLoop, calls=%fused_computation | loop fusion | flops 4194304 | bytes 12591104 | tf_op jit(solution)/shard_map/reshape;transpose | solution.py:374
  237.3 0.6 select_reduce_fusion
  (33 shorter events, 1.2 us)
Async XLA Ops:
  7.2 131.5 %reduce-scatter.3.cloned.1.call-start = ((), (), s32[]{:S(2)}) async-start(), calls=%async_computation.2 | async-start | bytes 5898240 | tf_op jit(solution)/shard_map/reduce_scatter | solution.py:293
  7.2 6.6 %collective-permute-start.1 = (bf16[16,256,256]{2,1,0:T(8,128)(2,1)}, bf16[16,256,256]{2,1,0:T(8,128)(2,1)S(1)}, u32[]{:S(2)}, u32[]{:S(2)}) collective-permute-start(bf16[16,256,256]{2,1,0:T(8,128)(2,1)} %bitcast.27), channel_id=1, source_target_pairs={{4,0},{8,4},{12,8},{16,12},{20,16},{24,20},{28,24},{5,1},{9,5},{13... | collective-permute-start | bytes 6291464 | tf_op jit(solution)/shard_map/ppermute | solution.py:267
  9.9 6.4 %collective-permute-start = (bf16[16,256,256]{2,1,0:T(8,128)(2,1)}, bf16[16,256,256]{2,1,0:T(8,128)(2,1)}, u32[]{:S(2)}, u32[]{:S(2)}) collective-permute-start(bf16[16,256,256]{2,1,0:T(8,128)(2,1)} %bitcast.28), channel_id=1, source_target_pairs={{0,4},{4,8},{8,12},{12,16},{16,20},{20,24},{24,28},{1,5},{5,9},{9,... | collective-permute-start | bytes 6291464 | tf_op jit(solution)/shard_map/ppermute | solution.py:266
  13.8 26.9 %copy-start.3 = (s32[1,32]{1,0:T(1,128)S(1)}, s32[1,32]{1,0:T(1,128)}, u32[]{:S(2)}) copy-start(s32[1,32]{1,0:T(1,128)} %param.15) | copy-start | bytes 388
  13.9 2.5 %copy-start.1 = (bf16[16,256,256]{2,1,0:T(8,128)(2,1)}, bf16[16,256,256]{2,1,0:T(8,128)(2,1)S(1)}, u32[]{:S(2)}) copy-start(bf16[16,256,256]{2,1,0:T(8,128)(2,1)S(1)} %collective-permute-done.1.above) | copy-start | bytes 6291460
  40.7 1.6 copy-start
  40.7 139.4 %reduce-scatter.5.cloned.1.call-start = ((), (), s32[]{:S(2)}) async-start(), calls=%async_computation.3 | async-start | bytes 1966080 | tf_op jit(solution)/shard_map/reduce_scatter | solution.py:330
  75.4 70.2 %copy-start.4 = (s32[1,32]{1,0:T(1,128)S(1)}, s32[1,32]{1,0:T(1,128)}, u32[]{:S(2)}) copy-start(s32[1,32]{1,0:T(1,128)} %param.14) | copy-start | bytes 388
  162.6 21.5 %copy-start.2 = (f32[8,128]{1,0:T(8,128)}, f32[8,128]{1,0:T(8,128)S(1)}, u32[]{:S(2)}) copy-start(f32[8,128]{1,0:T(8,128)S(1)} %scatter.9.labels) | copy-start | bytes 12292
Sparse Core Ops, SparseCore 0:
  40.8 97.7 reduce-scatter.2
  145.7 34.2 reduce-scatter.4

commit v3 on v2

--- a/solution.py
+++ b/solution.py
@@ -55,7 +55,7 @@
     return dot(table, jnp.concatenate((high, low, high), axis=0))
 
 
-def cut_kernel(info, below, here, above, boxes, sums, volume, window):
+def cut_kernel(info, below, here, above, boxes, sums, volume, first, second):
     depth, rows, cols = here.shape
     slots, box_len, _ = boxes.shape
     span = box_len + 16
@@ -68,8 +68,7 @@
     source = lax.broadcasted_iota(jnp.int32, (cols, 128), 0)
     quarter = lax.broadcasted_iota(jnp.int32, (box_len, 128), 1) // box_len
 
-    @pl.loop(0, slots)
-    def _(i):
+    def cut(i, window):
         z0 = info[0, i]
         x0 = info[1, i]
         y0 = info[2, i]
@@ -87,14 +86,13 @@
                 part = jnp.where(quarter == e, got, part)
             lanes = pl.ds(q * 128, 128)
             boxes[i, :, lanes] = part.astype(jnp.bfloat16)
-
-            @pl.when(live > 0)
-            def _():
-                sums[rot, :box_len, lanes] += part
-
-        @pl.when(live > 0)
-        def _():
-            sums[rot, box_len:, :] += 1.0
+            sums[rot, :box_len, lanes] += jnp.where(live > 0, part, 0.0)
+        sums[rot, box_len:, :] += jnp.where(live > 0, 1.0, 0.0)
+
+    @pl.loop(0, slots // 2)
+    def _(pair):
+        cut(2 * pair, first)
+        cut(2 * pair + 1, second)
 
 
 def score_kernel(rot, boxes, refs, ctf, plane, depth, out, spec, back_high, back_low):
@@ -286,6 +284,7 @@
         scratch_shapes=[
             pltpu.VMEM((2 * half + slab_depth, rows, cols), jnp.bfloat16),
             pltpu.VMEM((box_len * (box_len + 16), 128), jnp.float32),
+            pltpu.VMEM((box_len * (box_len + 16), 128), jnp.float32),
         ],
         compiler_params=pltpu.CompilerParams(vmem_limit_bytes=LIMIT),
     )(info, below, here, above)

time: 245 us -> 243 us (level)
    pallas_call x1, Pallas kernels: 24.3 us -> 21.6 us  [local(): pl.pallas_call(cut_kernel, out_shape=(jax.ShapeDtypeStruct((slots, box_le...]
where the time goes in v3:
time: 243 us; the launch traced here: 242 us
  Pallas kernels  117 us (48%)
  waiting for transfers between devices  83.2 us (34%)
  between operations  14.2 us (6%)
  other arithmetic  13.7 us (6%)
  local copies, waits for them, and re-layouts  10.2 us (4%)
  starting transfers between devices  4.09 us (2%)
    reduce_scatter x1, waiting for transfers between devices, local(): mine = lax.psum_scatter(sums, 'slab', scatter_dimension=0, tiled=True)  63.2 us
    pallas_call x2, Pallas kernels, score_part(): score_call(length)  45.5 us
    pallas_call x1, Pallas kernels, local(): pl.pallas_call(functools.partial(gather_kernel, slab_count, tomo_count),...  42.6 us
    pallas_call x1, Pallas kernels, local(): pl.pallas_call(cut_kernel, out_shape=(jax.ShapeDtypeStruct((slots, box_le...  21.6 us
    reduce_scatter x1, waiting for transfers between devices, local(): numer = lax.psum_scatter(spectra, 'tomo', scatter_dimension=1, tiled=True)  17.5 us
    pallas_call x1, Pallas kernels, local(): pl.pallas_call(class_kernel, out_shape=jax.ShapeDtypeStruct((3, count * b...  6.97 us
    another operation x1, other arithmetic, local(): jnp.swapaxes(decoded, 1, 2).reshape(ref_count, 2, box_len, cells)  5.69 us
  transfers between devices with their start and end apart: 4, of which 3 were waited for; matrix products, arithmetic and copies ran while one was open for 3% of the time, Pallas kernels for 19%

profile of v3, /device:TPU:15, one launch (start us, length us, event | category | flops | bytes accessed | tf_op | source)
XLA Modules:
  0.0 241.9 jit_solution(11571989184624257743)
XLA Ops:
  7.2 2.7 %collective-permute-start.1 = (bf16[16,256,256]{2,1,0:T(8,128)(2,1)}, bf16[16,256,256]{2,1,0:T(8,128)(2,1)S(1)}, u32[]{:S(2)}, u32[]{:S(2)}) collective-permute-start(bf16[16,256,256]{2,1,0:T(8,128)(2,1)} %bitcast.27), channel_id=1, source_target_pairs={{4,0},{8,4},{12,8},{16,12},{20,16},{24,20},{28,24},{5,1},{9,5},{13... | collective-permute-start | bytes 6291464 | tf_op jit(solution)/shard_map/ppermute | solution.py:265
  9.9 1.3 collective-permute-start
  11.2 0.7 compare_convert_fusion.1
  11.9 0.7 add_bitcast_fusion.1
  12.6 1.3 stack.2.info
  13.9 2.5 %collective-permute-done.below = bf16[16,256,256]{2,1,0:T(8,128)(2,1)} collective-permute-done((bf16[16,256,256]{2,1,0:T(8,128)(2,1)}, bf16[16,256,256]{2,1,0:T(8,128)(2,1)}, u32[]{:S(2)}, u32[]{:S(2)}) %collective-permute-start) | collective-permute-done | bytes 2097184 | tf_op jit(solution)/shard_map/ppermute | solution.py:264
  16.3 21.6 %shard_map.95 = (bf16[32,32,1024]{2,1,0:T(8,128)(2,1)}, f32[32,40,1024]{2,1,0:T(8,128)}) custom-call(s32[5,32]{1,0:T(8,128)} %stack.2.info, bf16[16,256,256]{2,1,0:T(8,128)(2,1)} %collective-permute-done.below, bf16[16,256,256]{2,1,0:T(8,128)(2,1)} %bitcast.29, bf16[16,256,256]{2,1,0:T(8,128)(2,1)} %copy-done.1), custom_call_target="tpu_custom_call" | custom-call | tf_op jit(solution)/shard_map/pallas_call | solution.py:276
  38.0 0.5 slice_bitcast_fusion.1.rot
  38.5 1.0 copy-done
  39.5 1.3 slice.97.boxes
  40.8 31.0 %shard_map.96 = f32[24,128]{1,0:T(8,128)} custom-call(s32[24]{0:T(128)} %slice_bitcast_fusion.1.rot, bf16[24,32,1024]{2,1,0:T(8,128)(2,1)} %slice.97.boxes, f32[32,2,32,1024]{3,2,1,0:T(8,128)} %refs.3, f32[32,1024]{1,0:T(8,128)} %bitcast.31, bf16[2,1024,2048]{2,1,0:T(8,128)(2,1)} %constant.104.clone.plane, bf16[2,64,192]{2,1,0:T(8,128)(2,1)} %constant.105.clone.depth), custom_call_target="tpu_custom_call" | custom-call | flops 25769803776 | bytes 20971520 | tf_op jit(solution)/shard_map/pallas_call | solution.py:310
  71.8 0.8 slice_reduce_fusion
  72.6 63.2 %reduce-scatter.3.cloned.1.call-done.sums = f32[4,40,1024]{2,1,0:T(8,128)} async-done(((f32[32,40,1024]{2,1,0:T(8,128)}), f32[4,40,1024]{2,1,0:T(8,128)}) %reduce-scatter.3.cloned.1.call-update) | async-done | bytes 655376 | tf_op jit(solution)/shard_map/reduce_scatter | solution.py:292
  135.8 7.0 %shard_map.97 = f32[3,128,1024]{2,1,0:T(8,128)} custom-call(f32[4,40,1024]{2,1,0:T(8,128)} %reduce-scatter.3.cloned.1.call-done.sums, f32[32,1024]{1,0:T(8,128)} %bitcast.32, bf16[2,1024,2048]{2,1,0:T(8,128)(2,1)} %constant.104.clone.plane, bf16[2,64,192]{2,1,0:T(8,128)(2,1)} %constant.105.clone.depth), custom_call_target="tpu_custom_call" | custom-call | flops 2147483648 | bytes 10485760 | tf_op jit(solution)/shard_map/pallas_call | solution.py:319
  142.8 0.6 slice_bitcast_fusion.rot
  143.4 0.8 slice.102.boxes
  144.3 14.5 %shard_map.98 = f32[8,128]{1,0:T(8,128)} custom-call(s32[8]{0:T(128)} %slice_bitcast_fusion.rot, bf16[8,32,1024]{2,1,0:T(8,128)(2,1)} %slice.102.boxes, f32[32,2,32,1024]{3,2,1,0:T(8,128)} %refs.3, f32[32,1024]{1,0:T(8,128)} %bitcast.33, bf16[2,1024,2048]{2,1,0:T(8,128)(2,1)} %constant.104.clone.plane, bf16[2,64,192]{2,1,0:T(8,128)(2,1)} %constant.105.clone.depth), custom_call_target="tpu_custom_call" | custom-call | flops 8589934592 | bytes 20971520 | tf_op jit(solution)/shard_map/pallas_call | solution.py:310
  158.7 0.8 slice_reduce_fusion.2
  159.8 17.5 %reduce-scatter.5.cloned.1.call-done = f32[3,32,1024]{2,1,0:T(8,128)} async-done(((f32[3,128,1024]{2,1,0:T(8,128)}), f32[3,32,1024]{2,1,0:T(8,128)}) %reduce-scatter.5.cloned.1.call-update) | async-done | bytes 393232 | tf_op jit(solution)/shard_map/reduce_scatter | solution.py:329
  177.3 0.9 fusion
  178.2 1.1 abs_reduce_fusion
  179.5 1.1 clamp_convert_fusion
  180.6 0.7 pad_add_fusion.chunk
  181.2 42.6 %shard_map.99 = (s16[8,4,64,1152]{3,2,1,0:T(8,128)(2,1)}, f32[8,8,128]{2,1,0:T(8,128)}) custom-call(s16[64,1152]{1,0:T(8,128)(2,1)} %pad_add_fusion.chunk, f32[8,128]{1,0:T(8,128)} %copy-done.2), custom_call_target="tpu_custom_call" | custom-call | tf_op jit(solution)/shard_map/pallas_call | solution.py:350
  223.9 0.8 compare_reduce_fusion
  224.7 0.8 fusion.6
  225.5 0.8 slice_reduce_fusion.1
  226.5 0.3 reduce-window.9
  227.1 1.1 slice.116
  228.2 0.5 copy.14
  228.8 5.7 %multiply_bitcast_fusion = f32[32,2,32,1024]{3,2,1,0:T(8,128)} fusion(s16[32,1,2,32,1152]{4,3,2,0,1:T(8,128)(2,1)} %bitcast.26, f32[32,2,32]{2,1,0:T(2,128)S(1)} %copy.13), kind=kLoop, calls=%fused_computation | loop fusion | flops 4194304 | bytes 12591104 | tf_op jit(solution)/shard_map/reshape;transpose | solution.py:373
  234.4 0.6 select_reduce_fusion
  (33 shorter events, 1.2 us)
Async XLA Ops:
  7.2 128.6 %reduce-scatter.3.cloned.1.call-start = ((), (), s32[]{:S(2)}) async-start(), calls=%async_computation.2 | async-start | bytes 5898240 | tf_op jit(solution)/shard_map/reduce_scatter | solution.py:292
  7.2 6.6 %collective-permute-start.1 = (bf16[16,256,256]{2,1,0:T(8,128)(2,1)}, bf16[16,256,256]{2,1,0:T(8,128)(2,1)S(1)}, u32[]{:S(2)}, u32[]{:S(2)}) collective-permute-start(bf16[16,256,256]{2,1,0:T(8,128)(2,1)} %bitcast.27), channel_id=1, source_target_pairs={{4,0},{8,4},{12,8},{16,12},{20,16},{24,20},{28,24},{5,1},{9,5},{13... | collective-permute-start | bytes 6291464 | tf_op jit(solution)/shard_map/ppermute | solution.py:265
  9.9 6.4 %collective-permute-start = (bf16[16,256,256]{2,1,0:T(8,128)(2,1)}, bf16[16,256,256]{2,1,0:T(8,128)(2,1)}, u32[]{:S(2)}, u32[]{:S(2)}) collective-permute-start(bf16[16,256,256]{2,1,0:T(8,128)(2,1)} %bitcast.28), channel_id=1, source_target_pairs={{0,4},{4,8},{8,12},{12,16},{16,20},{20,24},{24,28},{1,5},{5,9},{9,... | collective-permute-start | bytes 6291464 | tf_op jit(solution)/shard_map/ppermute | solution.py:264
  13.8 24.1 %copy-start.3 = (s32[1,32]{1,0:T(1,128)S(1)}, s32[1,32]{1,0:T(1,128)}, u32[]{:S(2)}) copy-start(s32[1,32]{1,0:T(1,128)} %param.15) | copy-start | bytes 388
  13.9 2.5 %copy-start.1 = (bf16[16,256,256]{2,1,0:T(8,128)(2,1)}, bf16[16,256,256]{2,1,0:T(8,128)(2,1)S(1)}, u32[]{:S(2)}) copy-start(bf16[16,256,256]{2,1,0:T(8,128)(2,1)S(1)} %collective-permute-done.1.above) | copy-start | bytes 6291460
  37.9 1.6 copy-start
  37.9 139.3 %reduce-scatter.5.cloned.1.call-start = ((), (), s32[]{:S(2)}) async-start(), calls=%async_computation.3 | async-start | bytes 1966080 | tf_op jit(solution)/shard_map/reduce_scatter | solution.py:329
  72.6 70.2 %copy-start.4 = (s32[1,32]{1,0:T(1,128)S(1)}, s32[1,32]{1,0:T(1,128)}, u32[]{:S(2)}) copy-start(s32[1,32]{1,0:T(1,128)} %param.14) | copy-start | bytes 388
  159.7 21.5 %copy-start.2 = (f32[8,128]{1,0:T(8,128)}, f32[8,128]{1,0:T(8,128)S(1)}, u32[]{:S(2)}) copy-start(f32[8,128]{1,0:T(8,128)S(1)} %scatter.9.labels) | copy-start | bytes 12292
Sparse Core Ops, SparseCore 0:
  38.1 97.7 reduce-scatter.2
  142.9 34.2 reduce-scatter.4
